TPU v7x, 512 devices: a whole 4x4x16 slice. The times are simulated.
512 devices in a mesh: dp: 32 (over y, x, core), owner: 16 (over z).
Axes of the slice: x: 4, y: 4, z: 16, core: 2. Of those that a mesh axis runs over, the one named last changes fastest.
Arguments:
- partials: float32 [32, 256, 256, 256], P('dp', None, 'owner'), may hold values from -0.125 to 0.125
- statistics: float32 [256, 2, 256, 256], P('dp', None, 'owner'), may hold values from -250 to 250, as said below
- assignment: int32 [512, 1], replicated, may hold values from 0 to 15; in each aligned block of 16 rows (0 to 15, 16 to 31, ...) at most 2 rows name the same one
Outputs:
- preconditioned: float32 [256, 256, 256], P('dp', 'owner')
- new_statistics: float32 [256, 2, 256, 256], P('dp', None, 'owner')
- stored_roots: bfloat16 [32, 16, 2, 256, 256], P('dp', 'owner')
Inputs may be any that keep to these rules, and one draw needn't show every extreme that they name: `assignment`: among the 16 matrices of one dp index (rows 16 k to 16 k + 15) no root owner appears more than 2 times, and 2 is reached in some dp index; every root owner appears somewhere. Every matrix statistics[b, k] is symmetric positive definite.
All inputs are finite; a program needn't handle non-finite values.
Results may differ from a plain program's by a relative error of at most 0.0014.
Values may be sent and summed in bfloat16 or wider, within the bound.
A program may use at most 128 MiB of HBM per device.

v0:
```python
import jax
import jax.numpy as jnp
from jax import lax
from jax.sharding import PartitionSpec as P

ITERS = 7


def batched(first, second):
    return jnp.einsum("nij,njk->nik", first, second, precision=lax.Precision.HIGHEST)


def inverse_root(matrices):
    order = matrices.shape[-1]
    unit_matrix = jnp.eye(order, dtype=jnp.float32)
    magnitude = jnp.sqrt(jnp.sum(matrices * matrices, axis=(1, 2)) + 1e-06)[:, None, None]
    current = matrices / magnitude
    result = current
    for iteration in range(ITERS):
        factor = (5.0 * unit_matrix - current) * 0.25
        if iteration == 0:
            result = factor * magnitude ** (-0.25)
        else:
            result = batched(result, factor)
        if iteration + 1 < ITERS:
            square = batched(factor, factor)
            current = batched(batched(square, square), current)
    return result


def root_items(received):
    return inverse_root(received[0])[None]


def place_rows(selector, pieces):
    return jnp.einsum("osj,jrc->osrc", selector, pieces, precision=lax.Precision.HIGHEST)


def pick_rows(selector, pieces):
    return jnp.einsum("osj,osrc->jrc", selector, pieces, precision=lax.Precision.HIGHEST)


def shards(partials, statistics, assignment):
    blocks = statistics.shape[0]
    row_count = statistics.shape[2]
    order = statistics.shape[3]
    stat_count = 2 * blocks
    owners = lax.axis_size("owner")
    slot_limit = max(2, 2 * stat_count // owners)
    owner_index = lax.axis_index("owner")
    dp_index = lax.axis_index("dp")
    summed = lax.psum_scatter(partials, "dp", scatter_dimension=1, tiled=True)[0]
    gathered = lax.all_gather(summed, "owner", axis=1, tiled=True)
    columns = lax.dynamic_slice_in_dim(gathered, owner_index * row_count, row_count, 2)
    left_new = statistics[:, 0] + jnp.einsum(
        "brk,bsk->brs", summed, gathered, precision=lax.Precision.HIGHEST
    )
    right_new = statistics[:, 1] + jnp.einsum(
        "bkr,bks->brs", columns, gathered, precision=lax.Precision.HIGHEST
    )
    new_statistics = jnp.stack([left_new, right_new], axis=1)
    my_owners = lax.dynamic_slice_in_dim(assignment[:, 0], dp_index * stat_count, stat_count)
    positions = jnp.arange(stat_count, dtype=jnp.int32)
    earlier = (my_owners[:, None] == my_owners[None, :]) & (positions[:, None] < positions[None, :])
    ranks = jnp.sum(earlier.astype(jnp.int32), axis=0)
    slot_ids = jnp.arange(slot_limit, dtype=jnp.int32)
    owner_ids = jnp.arange(owners, dtype=jnp.int32)
    placing = (
        (my_owners[None, None, :] == owner_ids[:, None, None])
        & (ranks[None, None, :] == slot_ids[None, :, None])
    ).astype(jnp.float32)
    slices = statistics.reshape(stat_count, row_count, order)
    outgoing = place_rows(placing, slices)
    roots_here = root_items(
        lax.all_to_all(outgoing, "owner", split_axis=0, concat_axis=2, tiled=True)
    )
    held_count = jnp.sum((my_owners == owner_index).astype(jnp.int32))
    live = (slot_ids < held_count).astype(jnp.float32)
    kept = (roots_here[0] * live[:, None, None]).astype(jnp.bfloat16)
    returned = lax.all_to_all(roots_here, "owner", split_axis=2, concat_axis=0, tiled=True)
    root_rows = pick_rows(placing, returned)
    root_pairs = root_rows.reshape(blocks, 2, row_count, order)
    right_full = lax.all_gather(root_pairs[:, 1], "owner", axis=1, tiled=True)
    shaped = jnp.einsum("brk,bks->brs", root_pairs[:, 0], gathered, precision=lax.Precision.HIGHEST)
    preconditioned = jnp.einsum("brk,bks->brs", shaped, right_full, precision=lax.Precision.HIGHEST)
    stored_roots = kept[None, None]
    return (preconditioned, new_statistics, stored_roots)


def solution(mesh):
    placed = (P("dp", None, "owner", None), P("dp", None, "owner", None), P())
    return jax.shard_map(
        shards,
        mesh=mesh,
        in_specs=placed,
        out_specs=(
            P("dp", "owner", None),
            P("dp", None, "owner", None),
            P("dp", "owner", None, None, None),
        ),
        check_vma=False,
    )
```

profile of v0, /device:TPU:24, one launch (start us, length us, event | category | flops | bytes accessed | tf_op | source)
XLA Modules:
  0.0 307.6 jit_solution(4847301606108850795)
XLA Ops:
  7.2 1.4 fusion.81
  8.6 1.4 fusion.43
  10.1 1.1 copy.40
  11.2 15.2 %all-to-all-start = ((f32[16,2,16,256]{3,2,1,0:T(8,128)}), f32[16,2,16,256]{3,2,1,0:T(8,128)S(1)}, u32[]{:S(2)}, u32[]{:S(2)}) async-start(f32[16,2,16,256]{3,2,1,0:T(8,128)} %copy.40), calls=%async_computation | async-start | bytes 1048576 | tf_op jit(solution)/shard_map/all_to_all | solution.py:75
  26.4 0.7 reduce-scatter.2.cloned.1.call-update
  27.2 28.3 %all-to-all-done = f32[16,2,16,256]{3,2,1,0:T(8,128)S(1)} async-done(((f32[16,2,16,256]{3,2,1,0:T(8,128)}), f32[16,2,16,256]{3,2,1,0:T(8,128)S(1)}, u32[]{:S(2)}, u32[]{:S(2)}) %all-to-all-start) | async-done | bytes 524320 | tf_op jit(solution)/shard_map/all_to_all | solution.py:75
  55.5 0.2 fusion.26
  55.7 0.1 bitcast_divide_fusion
  55.8 0.7 fusion.27
  56.6 0.6 fusion.97
  57.2 0.7 fusion.98
  57.9 0.7 fusion.33
  58.6 0.7 fusion.99
  59.3 0.7 fusion.100
  59.9 0.7 fusion.34
  60.7 0.6 fusion.101
  61.3 0.7 fusion.102
  62.0 0.7 fusion.36
  62.7 0.7 fusion.103
  63.4 0.7 fusion.104
  64.1 0.7 fusion.38
  64.8 0.6 fusion.105
  65.5 0.7 fusion.106
  66.1 0.7 fusion.40
  66.9 0.7 fusion.29
  67.6 0.9 fusion.35
  68.5 69.0 %reduce-scatter.2.cloned.1.call-done = f32[1,8,16,256]{3,2,1,0:T(8,128)} async-done(((f32[1,256,16,256]{3,2,1,0:T(8,128)}), f32[1,8,16,256]{3,2,1,0:T(8,128)}) %reduce-scatter.2.cloned.1.call-update) | async-done | bytes 131088 | tf_op jit(solution)/shard_map/reduce_scatter | solution.py:52
  137.5 0.6 fusion.107
  138.1 0.7 fusion.37
  138.8 0.7 fusion.39
  139.5 0.7 fusion.41
  140.2 0.7 fusion.9
  140.9 0.7 fusion.108
  141.6 1.2 copy.42
  142.8 12.3 %all-to-all-start.1 = ((f32[1,2,256,256]{3,1,0,2:T(2,128)}), f32[1,2,256,256]{3,1,0,2:T(2,128)S(1)}, u32[]{:S(2)}, u32[]{:S(2)}) async-start(f32[1,2,256,256]{3,1,0,2:T(2,128)} %copy.42), calls=%async_computation.1 | async-start | bytes 1048576 | tf_op jit(solution)/shard_map/all_to_all | solution.py:80
  155.1 0.7 fusion.84
  156.2 30.0 %all-to-all-done.1 = f32[1,2,256,256]{3,1,0,2:T(2,128)S(1)} async-done(((f32[1,2,256,256]{3,1,0,2:T(2,128)}), f32[1,2,256,256]{3,1,0,2:T(2,128)S(1)}, u32[]{:S(2)}, u32[]{:S(2)}) %all-to-all-start.1) | async-done | bytes 524320 | tf_op jit(solution)/shard_map/all_to_all | solution.py:80
  186.2 0.7 convolution_bitcast_fusion
  186.9 0.7 slice_bitcast_fusion
  187.6 0.7 compare_convert_fusion
  188.2 0.8 fusion.42
  189.0 36.9 %all-gather.5.cloned.1.call-done = f32[1,8,256,256]{3,2,1,0:T(8,128)} async-done(((f32[1,8,16,256]{3,2,1,0:T(8,128)}), f32[1,8,256,256]{3,2,1,0:T(8,128)}) %all-gather.5.cloned.1.call-update) | async-done | bytes 2097168 | tf_op jit(solution)/shard_map/all_gather | solution.py:53
  226.0 4.2 %fusion.19 = f32[8,1,16,256]{3,2,0,1:T(8,128)S(1)} fusion(f32[1,8,256,256]{3,2,1,0:T(8,128)} %all-gather.5.cloned.1.call-done, s32[]{:T(128)S(6)} %select_n.7, f32[8,2,16,256]{3,2,1,0:T(8,128)S(1)} %copy-done.1), kind=kOutput, calls=%fused_computation.15 | convolution fusion | flops 100696064 | bytes 3407876 | tf_op jit(solution)/shard_map/bkr,bks->brs/dot_general | solution.py:58
  230.2 1.9 fusion.13
  232.1 0.7 copy.51
  232.8 1.1 fusion.6
  233.9 63.2 %all-gather.7.cloned.1.call-done = f32[8,1,256,256]{3,0,1,2:T(8,128)} async-done(((f32[8,1,16,256]{3,0,1,2:T(8,128)}), f32[8,1,256,256]{3,0,1,2:T(8,128)}) %all-gather.7.cloned.1.call-update) | async-done | bytes 2097168 | tf_op jit(solution)/shard_map/all_gather | solution.py:83
  297.2 3.9 %fusion = f32[8,16,256]{2,1,0:T(8,128)} fusion(f32[8,16,256]{2,1,0:T(8,128)S(1)} %fusion.6, f32[8,1,256,256]{3,0,1,2:T(8,128)} %all-gather.7.cloned.1.call-done), kind=kOutput, calls=%fused_computation | convolution fusion | flops 100663296 | bytes 2359296 | tf_op jit(solution)/shard_map/brk,bks->brs/dot_general | solution.py:85
  (24 shorter events, 0.8 us)
Async XLA Ops:
  11.2 44.3 %all-to-all-start = ((f32[16,2,16,256]{3,2,1,0:T(8,128)}), f32[16,2,16,256]{3,2,1,0:T(8,128)S(1)}, u32[]{:S(2)}, u32[]{:S(2)}) async-start(f32[16,2,16,256]{3,2,1,0:T(8,128)} %copy.40), calls=%async_computation | async-start | bytes 1048576 | tf_op jit(solution)/shard_map/all_to_all | solution.py:75
  26.4 111.1 %reduce-scatter.2.cloned.1.call-start = ((), (), s32[]{:S(2)}) async-start(), calls=%async_computation.3 | async-start | bytes 4325376 | tf_op jit(solution)/shard_map/reduce_scatter | solution.py:52
  27.1 198.8 %all-gather.5.cloned.1.call-start = ((), (), s32[]{:S(2)}) async-start(), calls=%async_computation.4 | async-start | bytes 2228224 | tf_op jit(solution)/shard_map/all_gather | solution.py:53
  141.5 84.4 %copy-start.1 = (f32[8,2,16,256]{3,2,1,0:T(8,128)S(1)}, f32[8,2,16,256]{3,2,1,0:T(8,128)}, u32[]{:S(2)}) copy-start(f32[8,2,16,256]{3,2,1,0:T(8,128)} %param.4) | copy-start | bytes 786436
  142.8 43.4 %all-to-all-start.1 = ((f32[1,2,256,256]{3,1,0,2:T(2,128)}), f32[1,2,256,256]{3,1,0,2:T(2,128)S(1)}, u32[]{:S(2)}, u32[]{:S(2)}) async-start(f32[1,2,256,256]{3,1,0,2:T(2,128)} %copy.42), calls=%async_computation.1 | async-start | bytes 1048576 | tf_op jit(solution)/shard_map/all_to_all | solution.py:80
  155.0 142.1 %all-gather.7.cloned.1.call-start = ((), (), s32[]{:S(2)}) async-start(), calls=%async_computation.5 | async-start | bytes 2228224 | tf_op jit(solution)/shard_map/all_gather | solution.py:83
  186.9 43.3 %copy-start.2 = (f32[1,8,16,256]{3,2,1,0:T(8,128)S(1)}, f32[1,8,16,256]{3,2,1,0:T(8,128)}, u32[]{:S(2)}) copy-start(f32[1,8,16,256]{3,2,1,0:T(8,128)} %reduce-scatter.2.cloned.1.call-done) | copy-start | bytes 393220
  226.0 4.2 %copy-start = (f32[1,8,256,256]{3,2,1,0:T(8,128)S(1)}, f32[1,8,256,256]{3,2,1,0:T(8,128)}, u32[]{:S(2)}) copy-start(f32[1,8,256,256]{3,2,1,0:T(8,128)} %all-gather.5.cloned.1.call-done) | copy-start | bytes 6291460
Sparse Core Ops, SparseCore 0:
  31.7 105.6 reduce-scatter.1
  139.8 86.1 all-gather.4
  228.8 68.2 all-gather.6
where the time goes:
time: 308 us
  waiting for transfers between devices  228 us (74%)
  matrix products  29.7 us (10%)
  starting transfers between devices  27.6 us (9%)
  between operations  14 us (5%)
  local copies, waits for them, and re-layouts  4.82 us (2%)
  other arithmetic  3.35 us (1%)
    reduce_scatter x1, waiting for transfers between devices, shards(): lax.psum_scatter(partials, 'dp', scatter_dimension=1, tiled=True)[0]  69 us
    all_gather x1, waiting for transfers between devices, shards(): right_full = lax.all_gather(root_pairs[:, 1], 'owner', axis=1, tiled=True)  63.2 us
    all_gather x1, waiting for transfers between devices, shards(): gathered = lax.all_gather(summed, 'owner', axis=1, tiled=True)  36.9 us
    all_to_all x1, waiting for transfers between devices, shards(): lax.all_to_all(roots_here, 'owner', split_axis=2, concat_axis=0, tiled=True)  30 us
    all_to_all x1, waiting for transfers between devices, shards(): lax.all_to_all(outgoing, 'owner', split_axis=0, concat_axis=2, tiled=True)  28.3 us
    dot_general x24, matrix products, batched(): jnp.einsum('nij,njk->nik', first, second, precision=lax.Precision.HIGHEST)  16.5 us
    all_to_all x1, starting transfers between devices, shards(): lax.all_to_all(outgoing, 'owner', split_axis=0, concat_axis=2, tiled=True)  15.2 us
    all_to_all x1, starting transfers between devices, shards(): lax.all_to_all(roots_here, 'owner', split_axis=2, concat_axis=0, tiled=True)  12.3 us
  transfers between devices with their start and end apart: 5, of which 5 were waited for; matrix products, arithmetic and copies ran while one was open for 10% of the time, Pallas kernels for 0%

commit v1 on v0

v1 whole, which is shorter than its diff:
```python
import jax
import jax.numpy as jnp
from jax import lax
from jax.experimental import pallas as pl
from jax.experimental.pallas import tpu as pltpu
from jax.sharding import PartitionSpec as P

MESH = pl.DeviceIdType.MESH
F32, BF16, I16, I32 = jnp.float32, jnp.bfloat16, jnp.int16, jnp.int32
NX = NY = 4
NZ = 16
NB = 8
ROWS = 16
N = 256
H = 128
ITERS = 7
LEVELS = 32760.0 / 32768.0
B_MSG, C_MSG, G_MSG, R_MSG = 33, 9, 17, 25
G_PARTS = ((0, 9), (9, 8))
R_PARTS = ((0, 13), (13, 12))


def code(x):
    return jnp.round(x).astype(I32).astype(I16)


def encode(x, dst):
    m = x.shape[0]
    left, right = x[:, :, :H], x[:, :, H:]
    top = jnp.maximum(jnp.max(jnp.abs(left), axis=0), jnp.max(jnp.abs(right), axis=0))
    e = jnp.ceil(jnp.log2(jnp.maximum(top, 1e-30)))
    up = (jnp.exp2(15.0 - e) * LEVELS)[None]
    dst[0:m] = code(left * up)
    dst[m : 2 * m] = code(right * up)
    dst[2 * m] = code(e)


def value(q):
    return q.astype(I32).astype(F32)


def unit(e):
    return jnp.exp2(value(e) - 15.0) * (1.0 / LEVELS)


def decode(src, m):
    down = unit(src[2 * m])[None]
    return value(src[0:m]) * down, value(src[m : 2 * m]) * down


def encode_root(x, dst):
    x = jnp.concatenate([x[:H, :H], x[:H, H:], x[H:, H:]], axis=0).reshape(24, ROWS, H)
    e = jnp.ceil(jnp.log2(jnp.maximum(jnp.max(jnp.abs(x), axis=0), 1e-30)))
    dst[0:24] = code(x * (jnp.exp2(15.0 - e) * LEVELS)[None])
    dst[24] = code(e)


def decode_root(q):
    v = (value(q[0:24]) * unit(q[24])[None]).reshape(3 * H, H)
    return v[:H], v[H : 2 * H], v[2 * H :]


def split(x):
    high = x.astype(BF16)
    return high, (x - high.astype(F32)).astype(BF16)


def dot(a, b):
    return jnp.dot(a, b, preferred_element_type=F32)


def dot_nt(a, b):
    return lax.dot_general(a, b, (((1,), (1,)), ((), ())), preferred_element_type=F32)


def dot3(a, b):
    (ah, al), (bh, bl) = a, b
    return dot(ah, bh) + (dot(al, bh) + dot(ah, bl))


def kernel(
    p_ref, s_ref, owner_ref, pre_ref, new_ref, kept_ref,
    srows, own, other, bsend, brecv, csend, crecv, acc, gown, smat, cur, root, gq, ghi, glo, rq,
    own_sem, stat_sem, a_send, a_recv, b_send, b_recv, c_send, c_recv, s_send, s_recv,
    g_right, g_left, g_recv, r_right, r_left, r_recv,
):
    dp = lax.axis_index("dp")
    z = lax.axis_index("owner")
    core = lax.rem(dp, 2)
    x = lax.rem(dp // 2, NX)
    y = dp // (2 * NX)

    def plane(yy, xx, cc):
        return ((yy * NX + xx) * 2 + cc, z)

    def column(zz):
        return (dp, zz)

    def step(i, k, n):
        return lax.rem(i + k, n)

    partner = plane(y, x, 1 - core)

    def along(half, k):
        return plane(y, step(x, k, NX), core) if half == 0 else plane(step(y, k, NY), x, core)

    barrier = pltpu.get_barrier_semaphore()
    for k in range(1, NZ):
        pl.semaphore_signal(barrier, inc=1, device_id=column(step(z, k, NZ)), device_id_type=MESH)
    pl.semaphore_signal(barrier, inc=1, device_id=partner, device_id_type=MESH)
    for half in range(2):
        for k in range(1, 4):
            pl.semaphore_signal(barrier, inc=1, device_id=along(half, k), device_id_type=MESH)
    pl.semaphore_wait(barrier, NZ - 1 + 1 + 6)

    def remote(src, dst, send, recv, to):
        return pltpu.make_async_remote_copy(
            src_ref=src, dst_ref=dst, send_sem=send, recv_sem=recv, device_id=to, device_id_type=MESH
        )

    def chunk(half, k, cc):
        if half == 0:
            return p_ref.at[:, step(x, k, NX), cc, pl.ds(0, 4)]
        return p_ref.at[step(y, k, NY), :, cc, pl.ds(4, 4)]

    def to_partner(half, k):
        return remote(
            chunk(half, k, 1 - core), other.at[half, k], a_send.at[half, k], a_recv.at[half, k], partner
        )

    def mine(half, k):
        return pltpu.make_async_copy(chunk(half, k, core), own.at[half, k], own_sem.at[half, k])

    def rows_to(k):
        to = step(z, k, NZ)
        return remote(s_ref.at[to], smat.at[z], s_send.at[k], s_recv.at[k], column(to))

    def rows_from(k):
        return remote(s_ref.at[z], smat.at[step(z, NZ - k, NZ)], s_send.at[k], s_recv.at[k], column(step(z, k, NZ)))

    ORDER = (2, 1, 3, 0)
    for half in range(2):
        to_partner(half, 2).start()
        mine(half, 2).start()
    for k in (8, 7, 9, 6, 10, 5, 11, 4, 12, 3, 13, 2, 14, 1, 15):
        rows_to(k).start()
    for k in ORDER[1:]:
        for half in range(2):
            to_partner(half, k).start()
            mine(half, k).start()
    own_rows = pltpu.make_async_copy(s_ref.at[z], smat.at[z], s_recv.at[0])
    own_rows.start()
    all_rows = pltpu.make_async_copy(s_ref, srows, stat_sem)
    all_rows.start()

    def b_copy(half, k):
        return remote(bsend.at[half, k - 1], brecv.at[half, k - 1], b_send.at[half, k - 1], b_recv.at[half, k - 1], along(half, k))

    def c_copy(half, k):
        return remote(csend.at[half, k - 1], crecv.at[half, k - 1], c_send.at[half, k - 1], c_recv.at[half, k - 1], along(1 - half, k))

    for k in ORDER:
        for half in range(2):
            to_partner(half, k).wait_recv()
            mine(half, k).wait()
            total = own[half, k] + other[half, k]
            if k:
                encode(total.reshape(16, ROWS, N), bsend.at[half, k - 1])
                b_copy(half, k).start()
            else:
                acc[half] = total

    right_z, left_z = column(step(z, 1, NZ)), column(step(z, NZ - 1, NZ))

    def ring(buf, parts, right_sem, left_sem, recv):
        def hop(d, s, p):
            origin = step(z, NZ - s, NZ) if d == 0 else step(z, s, NZ)
            at = buf.at[origin, pl.ds(*parts[p])]
            sem = (right_sem if d == 0 else left_sem).at[s, p]
            return remote(at, at, sem, recv.at[origin, p], right_z if d == 0 else left_z)

        def arrive(d, s, p, forward):
            c = hop(d, s, p)
            c.wait_recv()
            if forward:
                c.start()

        def begin():
            for p in range(2):
                for d in range(2):
                    hop(d, 0, p).start()

        def finish():
            for p in range(2):
                for s in range(8):
                    hop(0, s, p).wait_send()
                for s in range(7):
                    hop(1, s, p).wait_send()

        return arrive, begin, finish

    g_arrive, g_begin, g_finish = ring(gq, G_PARTS, g_right, g_left, g_recv)
    r_arrive, r_begin, r_finish = ring(rq, R_PARTS, r_right, r_left, r_recv)

    def unpack_g(origin):
        a, b = decode(gq.at[origin], NB)
        ah, al = split(a)
        bh, bl = split(b)
        ghi[origin, :, :, :H] = ah
        ghi[origin, :, :, H:] = bh
        glo[origin, :, :, :H] = al
        glo[origin, :, :, H:] = bl

    def plane_sums():
        for half in range(2):
            left = acc[half, :, :, :, :H].reshape(16, ROWS, H)
            right = acc[half, :, :, :, H:].reshape(16, ROWS, H)
            for k in (1, 3, 2):
                b_copy(half, k).wait_recv()
                a, b = decode(brecv.at[half, k - 1], 16)
                left, right = left + a, right + b
            acc[half, :, :, :, :H] = left.reshape(4, 4, ROWS, H)
            acc[half, :, :, :, H:] = right.reshape(4, 4, ROWS, H)
            me = y if half == 0 else x
            for k in (2, 1, 3):
                encode(acc[half, step(me, k, 4)], csend.at[half, k - 1])
                c_copy(half, k).start()


    def own_sums():
        for half in range(2):
            me = y if half == 0 else x
            g = acc[half, me]
            left, right = g[:, :, :H], g[:, :, H:]
            for k in (1, 3, 2):
                c_copy(half, k).wait_recv()
                a, b = decode(crecv.at[half, k - 1], 4)
                left, right = left + a, right + b
            gown[pl.ds(4 * half, 4), :, :H] = left
            gown[pl.ds(4 * half, 4), :, H:] = right

    def unpack_g(origin):
        a, b = decode(gq.at[origin], NB)
        ah, al = split(a)
        bh, bl = split(b)
        ghi[origin, :, :, :H] = ah
        ghi[origin, :, :, H:] = bh
        glo[origin, :, :, :H] = al
        glo[origin, :, :, H:] = bl

    def g_step(s):
        for p in range(2):
            g_arrive(0, s, p, s < 8)
            if s < 8:
                g_arrive(1, s, p, s < 7)

    def unpack_step(s):
        unpack_g(step(z, NZ - s, NZ))
        if s < 8:
            unpack_g(step(z, s, NZ))

    def iteration():
        current = cur[...]
        f = factor_of(current)
        fs, rs = split(f), split(root[...])
        both = tuple(jnp.concatenate([u, v], axis=0) for u, v in zip(fs, rs))
        product = dot3(both, fs)
        root[...] = product[N:]
        cur[...] = powered(fs, product[:N], current)

    own_rows.wait()
    for k in range(1, NZ):
        rows_from(k).wait_recv()
    eye = (lax.broadcasted_iota(I32, (N, N), 0) == lax.broadcasted_iota(I32, (N, N), 1)).astype(F32)

    def factor_of(current):
        return (5.0 * eye - current) * 0.25

    def powered(f, square, current):
        s = split(square)
        q = dot3(s, s)
        return dot3(split(q), split(current))

    matrix = smat[...].reshape(N, N)
    magnitude = jnp.sqrt(jnp.sum(matrix * matrix, keepdims=True) + 1e-6)
    current = matrix / magnitude
    f = factor_of(current)
    root[...] = f * lax.rsqrt(jnp.sqrt(magnitude))
    fs = split(f)
    cur[...] = powered(fs, dot3(fs, fs), current)

    plane_sums()
    iteration()
    own_sums()
    encode(gown[...], gq.at[z])
    g_begin()
    iteration()
    iteration()
    g_step(1)
    iteration()
    g_step(2)
    iteration()
    last = dot3(split(root[...]), split(factor_of(cur[...])))
    encode_root(last, rq.at[z])
    r_begin()

    def r_step(s, *units):
        units = units + (None,) * 4
        for i, (p, d) in enumerate(((0, 0), (0, 1), (1, 0), (1, 1))):
            if s < 8 or d == 0:
                r_arrive(d, s, p, s < 8 - d)
            if units[i] is not None:
                units[i]()

    unpack_g(z)
    unpack_step(1)
    for s in range(1, 4):
        g_step(2 * s + 1)
        unpack_step(2 * s)
        r_step(s)
        g_step(2 * s + 2)
        unpack_step(2 * s + 1)
    unpack_step(8)
    all_rows.wait()

    pick = (
        lax.broadcasted_iota(I32, (ROWS, N), 1) == lax.broadcasted_iota(I32, (ROWS, N), 0) + z * ROWS
    ).astype(F32).astype(BF16)

    def halves(b):
        return ghi[:, b].reshape(N, N), glo[:, b].reshape(N, N)

    def statistics(b):
        gh, gl = halves(b)
        rh, rl = split(gown[b])
        one = dot_nt(jnp.concatenate([rh, rl, pick], axis=0), gh)
        two = dot_nt(jnp.concatenate([rh, pick], axis=0), gl)
        new_ref[2 * b] = srows[2 * b] + one[:16] + (one[16:32] + two[:16])
        ch, cl = one[32:48].astype(BF16), two[16:32].astype(BF16)
        three = dot(jnp.concatenate([ch, cl], axis=0), gh)
        new_ref[2 * b + 1] = srows[2 * b + 1] + three[:16] + (three[16:32] + dot(ch, gl))

    pick_low = (
        lax.broadcasted_iota(I32, (ROWS, H), 1)
        == lax.broadcasted_iota(I32, (ROWS, H), 0) + (z - 8) * ROWS
    ).astype(F32).astype(BF16)

    def precondition(t):
        b = step(pair, t, NB)
        gh, gl = halves(b)
        q = rq[2 * b]
        down = unit(q[24])
        bh, bl = split((value(q[8:16]) * down[None]).reshape(H, H))
        upper = value(rq[2 * b, lax.rem(z, 8)]) * down
        lower = dot_nt(pick_low, bh) + dot_nt(pick_low, bl)
        rows = jnp.concatenate([jnp.where(z < 8, upper, lower), value(rq[2 * b, 8 + z]) * down], axis=1)
        lh, ll = split(rows)
        shaped = dot(jnp.concatenate([lh, ll], axis=0), gh)
        shaped = shaped[:16] + (shaped[16:] + dot(lh, gl))
        a, c, d = decode_root(rq[2 * b + 1])
        right = jnp.concatenate(
            [jnp.concatenate([a, c], axis=1), jnp.concatenate([c.T, d], axis=1)], axis=0
        )
        rh, rl = split(right)
        sh, sl = split(shaped)
        out = dot(jnp.concatenate([sh, sl], axis=0), rh)
        pre_ref[b] = out[:16] + (out[16:] + dot(sh, rl))

    pair = z // 2

    def stat(b):
        return lambda: statistics(b)

    def pre(t):
        return lambda: precondition(t)

    r_step(4, stat(0), stat(1), pre(0), stat(2))
    r_step(5, stat(3), pre(1), stat(4), pre(7))
    r_step(6, stat(5), pre(2), stat(6), pre(6))
    r_step(7, stat(7))
    r_step(8, pre(3), None, pre(5))
    precondition(4)

    first, second, count = jnp.int32(0), jnp.int32(0), jnp.int32(0)
    for j in range(16):
        hit = owner_ref[dp * 16 + j] == z
        first = jnp.where(hit & (count == 0), j, first)
        second = jnp.where(hit & (count == 1), j, second)
        count = count + hit.astype(I32)
    for slot, j in enumerate((first, second)):
        live = (count > slot).astype(F32)
        a, c, d = decode_root(rq[j])
        kept_ref[slot, 0:8, :, :H] = (a * live).astype(BF16).reshape(8, ROWS, H)
        kept_ref[slot, 0:8, :, H:] = (c * live).astype(BF16).reshape(8, ROWS, H)
        kept_ref[slot, 8:16, :, :H] = (c.T * live).astype(BF16).reshape(8, ROWS, H)
        kept_ref[slot, 8:16, :, H:] = (d * live).astype(BF16).reshape(8, ROWS, H)

    for half in range(2):
        for k in range(4):
            to_partner(half, k).wait_send()
        for k in range(1, 4):
            b_copy(half, k).wait_send()
            c_copy(half, k).wait_send()
    for k in range(1, NZ):
        rows_to(k).wait_send()
    g_finish()
    r_finish()


def shards(partials, statistics, assignment):
    vmem, dma = pltpu.VMEM, pltpu.SemaphoreType.DMA
    pre, new, kept = pl.pallas_call(
        kernel,
        out_shape=(
            jax.ShapeDtypeStruct((NB, ROWS, N), F32),
            jax.ShapeDtypeStruct((2 * NB, ROWS, N), F32),
            jax.ShapeDtypeStruct((2, 16, 16, N), BF16),
        ),
        in_specs=[
            pl.BlockSpec(memory_space=pl.ANY),
            pl.BlockSpec(memory_space=pl.ANY),
            pl.BlockSpec(memory_space=pltpu.SMEM),
        ],
        out_specs=[pl.BlockSpec(memory_space=pltpu.VMEM)] * 3,
        scratch_shapes=[
            vmem((2 * NB, ROWS, N), F32),
            vmem((2, 4, 4, 4, ROWS, N), F32),
            vmem((2, 4, 4, 4, ROWS, N), F32),
            vmem((2, 3, B_MSG, ROWS, H), I16),
            vmem((2, 3, B_MSG, ROWS, H), I16),
            vmem((2, 3, C_MSG, ROWS, H), I16),
            vmem((2, 3, C_MSG, ROWS, H), I16),
            vmem((2, 4, 4, ROWS, N), F32),
            vmem((NB, ROWS, N), F32),
            vmem((NZ, ROWS, N), F32),
            vmem((N, N), F32),
            vmem((N, N), F32),
            vmem((NZ, G_MSG, ROWS, H), I16),
            vmem((NZ, NB, ROWS, N), BF16),
            vmem((NZ, NB, ROWS, N), BF16),
            vmem((NZ, R_MSG, ROWS, H), I16),
            dma((2, 4)), dma, dma((2, 4)), dma((2, 4)),
            dma((2, 3)), dma((2, 3)), dma((2, 3)), dma((2, 3)),
            dma((NZ,)), dma((NZ,)),
            dma((8, 2)), dma((7, 2)), dma((NZ, 2)),
            dma((8, 2)), dma((7, 2)), dma((NZ, 2)),
        ],
        compiler_params=pltpu.CompilerParams(
            collective_id=0, has_side_effects=True, vmem_limit_bytes=60 * 1024 * 1024
        ),
        cost_estimate=pl.CostEstimate(flops=3_000_000_000, bytes_accessed=6_000_000, transcendentals=0),
    )(
        partials.reshape(NY, NX, 2, NB, ROWS, N),
        statistics.reshape(2 * NB, ROWS, N),
        assignment.reshape(-1),
    )
    return pre, new.reshape(NB, 2, ROWS, N), kept.reshape(1, 1, 2, N, N)


def solution(mesh):
    placed = (P("dp", None, "owner", None), P("dp", None, "owner", None), P())
    return jax.shard_map(
        shards,
        mesh=mesh,
        in_specs=placed,
        out_specs=(
            P("dp", "owner", None),
            P("dp", None, "owner", None),
            P("dp", "owner", None, None, None),
        ),
        check_vma=False,
    )
```

time: 308 us -> 94 us (0.31)
  waiting for transfers between devices: 228 us -> 0 us
  Pallas kernels: 0 us -> 88.2 us
  matrix products: 29.7 us -> 0 us
  starting transfers between devices: 27.6 us -> 0 us
  between operations: 14 us -> 0.64 us
  other arithmetic: 3.35 us -> 0 us
    all_gather x2 -> x0, waiting for transfers between devices: 100 us -> none  [the longest x1 63.2 us: shards(): right_full = lax.all_gather(root_pairs[:, 1], 'owner', axis=1, tiled=True)]
    pallas_call x0 -> x1, Pallas kernels: none -> 88.2 us  [shards(): pl.pallas_call(kernel, out_shape=(jax.ShapeDtypeStruct((NB, ROWS, N), F32...]
    reduce_scatter x1 -> x0, waiting for transfers between devices: 69 us -> none  [shards(): lax.psum_scatter(partials, 'dp', scatter_dimension=1, tiled=True)[0]]
    all_to_all x2 -> x0, waiting for transfers between devices: 58.3 us -> none  [the longest x1 30 us: shards(): lax.all_to_all(roots_here, 'owner', split_axis=2, concat_axis=0, tiled=True)]
    dot_general x30 -> x0, matrix products: 29.7 us -> none  [the longest x24 16.5 us: batched(): jnp.einsum('nij,njk->nik', first, second, precision=lax.Precision.HIGHEST)]
    all_to_all x2 -> x0, starting transfers between devices: 27.5 us -> none  [the longest x1 15.2 us: shards(): lax.all_to_all(outgoing, 'owner', split_axis=0, concat_axis=2, tiled=True)]
    unnamed x7 -> x3, local copies, waits for them, and re-layouts: 0.74 us -> 4.91 us
  transfers between devices with their start and end apart: 5 -> 0, of which waited for: 5 -> 0; matrix products, arithmetic and copies ran while one was open for 10% -> 0% of each run, Pallas kernels for 0% -> 0%
where the time goes in v1:
time: 94 us; the launch traced here: 93.7 us
  Pallas kernels  88.2 us (94%)
  local copies, waits for them, and re-layouts  4.91 us (5%)
    pallas_call x1, Pallas kernels, shards(): pl.pallas_call(kernel, out_shape=(jax.ShapeDtypeStruct((NB, ROWS, N), F32...  88.2 us
    unnamed x3, local copies, waits for them, and re-layouts  4.91 us

profile of v1, /device:TPU:24, one launch (start us, length us, event | category | flops | bytes accessed | tf_op | source)
XLA Modules:
  0.0 93.7 jit_solution(7361801035651842537)
XLA Ops:
  0.6 88.2 %shard_map.58 = (f32[8,16,256]{2,1,0:T(8,128)}, f32[16,16,256]{2,1,0:T(8,128)}, bf16[2,16,16,256]{3,2,1,0:T(8,128)(2,1)}) custom-call(f32[4,4,2,8,16,256]{5,4,3,2,1,0:T(8,128)} %bitcast.7, f32[16,16,256]{2,1,0:T(8,128)} %bitcast.8, s32[512]{0:T(512)} %bitcast.9), custom_call_target="tpu_custom_call" | custom-call | flops 3000000000 | bytes 6000000 | tf_op jit(solution)/shard_map/pallas_call | solution.py:412
  88.8 1.6 %copy.9 = f32[8,16,256]{2,1,0:T(8,128)} copy(f32[8,16,256]{2,1,0:T(8,128)} %get-tuple-element.12) | data formatting | bytes 262144
  90.4 1.7 %copy.10 = f32[8,2,16,256]{3,2,1,0:T(8,128)} copy(f32[8,2,16,256]{3,2,1,0:T(8,128)} %bitcast.6) | data formatting | bytes 524288
  92.1 1.7 %copy.11 = bf16[1,1,2,256,256]{4,3,2,1,0:T(8,128)(2,1)} copy(bf16[1,1,2,256,256]{4,3,2,1,0:T(8,128)(2,1)} %bitcast.5) | data formatting | bytes 524288

commit v2 on v1

--- a/solution.py
+++ b/solution.py
@@ -15,7 +15,7 @@
 H = 128
 ITERS = 7
 LEVELS = 32760.0 / 32768.0
-B_MSG, C_MSG, G_MSG, R_MSG = 33, 9, 17, 25
+A_MSG, B_MSG, C_MSG, G_MSG, R_MSG = 33, 17, 9, 17, 25
 G_PARTS = ((0, 9), (9, 8))
 R_PARTS = ((0, 13), (13, 12))
 
@@ -24,9 +24,9 @@
     return jnp.round(x).astype(I32).astype(I16)
 
 
-def encode(x, dst):
-    m = x.shape[0]
-    left, right = x[:, :, :H], x[:, :, H:]
+def encode(halves, dst):
+    left, right = halves
+    m = left.shape[0]
     top = jnp.maximum(jnp.max(jnp.abs(left), axis=0), jnp.max(jnp.abs(right), axis=0))
     e = jnp.ceil(jnp.log2(jnp.maximum(top, 1e-30)))
     up = (jnp.exp2(15.0 - e) * LEVELS)[None]
@@ -79,9 +79,9 @@
 
 
 def kernel(
-    p_ref, s_ref, owner_ref, pre_ref, new_ref, kept_ref,
-    srows, own, other, bsend, brecv, csend, crecv, acc, gown, smat, cur, root, gq, ghi, glo, rq,
-    own_sem, stat_sem, a_send, a_recv, b_send, b_recv, c_send, c_recv, s_send, s_recv,
+    p_ref, s_ref, pre_ref, new_ref, rq,
+    srows, own, theirs, asend, arecv, bsend, brecv, csend, crecv, gown, smat, cur, root, gq, ghi, glo,
+    own_sem, their_sem, stat_sem, a_send, a_recv, b_send, b_recv, c_send, c_recv, s_send, s_recv,
     g_right, g_left, g_recv, r_right, r_left, r_recv,
 ):
     dp = lax.axis_index("dp")
@@ -111,7 +111,6 @@
     for half in range(2):
         for k in range(1, 4):
             pl.semaphore_signal(barrier, inc=1, device_id=along(half, k), device_id_type=MESH)
-    pl.semaphore_wait(barrier, NZ - 1 + 1 + 6)
 
     def remote(src, dst, send, recv, to):
         return pltpu.make_async_remote_copy(
@@ -124,37 +123,80 @@
         return p_ref.at[step(y, k, NY), :, cc, pl.ds(4, 4)]
 
     def to_partner(half, k):
-        return remote(
-            chunk(half, k, 1 - core), other.at[half, k], a_send.at[half, k], a_recv.at[half, k], partner
-        )
-
-    def mine(half, k):
-        return pltpu.make_async_copy(chunk(half, k, core), own.at[half, k], own_sem.at[half, k])
-
-    def rows_to(k):
-        to = step(z, k, NZ)
-        return remote(s_ref.at[to], smat.at[z], s_send.at[k], s_recv.at[k], column(to))
-
-    def rows_from(k):
-        return remote(s_ref.at[z], smat.at[step(z, NZ - k, NZ)], s_send.at[k], s_recv.at[k], column(step(z, k, NZ)))
+        return remote(asend.at[half, k], arecv.at[half, k], a_send.at[half, k], a_recv.at[half, k], partner)
+
+    def load(half, k, cc, dst, sem):
+        return pltpu.make_async_copy(chunk(half, k, cc), dst.at[half, k], sem.at[half, k])
+
+    def load_mine(half, k):
+        return load(half, k, core, own, own_sem)
+
+    def load_theirs(half, k):
+        return load(half, k, 1 - core, theirs, their_sem)
+
+    def rows(k, source, to, run):
+        at = column(step(z, k, NZ))
+        whole = lax.rem(source // 8 + to, 2) == 0
+        part = pl.ds(pl.multiple_of((source // 8) * H, H), H)
+
+        @pl.when(whole)
+        def _():
+            run(remote(s_ref.at[to], smat.at[source], s_send.at[k], s_recv.at[k], at))
+
+        @pl.when(jnp.logical_not(whole))
+        def _():
+            run(remote(s_ref.at[to, :, part], smat.at[source, :, part], s_send.at[k], s_recv.at[k], at))
+
+    def rows_to(k, run):
+        rows(k, z, step(z, k, NZ), run)
+
+    def rows_from(k, run):
+        rows(k, step(z, NZ - k, NZ), z, run)
 
     ORDER = (2, 1, 3, 0)
-    for half in range(2):
-        to_partner(half, 2).start()
-        mine(half, 2).start()
+
+    def halves_of(ref, half, k, first, count):
+        at = ref.at[half, k, pl.ds(first, count)]
+        return tuple(at[:, :, :, i : i + H].reshape(count * 4, ROWS, H) for i in (0, H))
+
+    def put(ref, half, k, first, count, halves):
+        at = ref.at[half, k, pl.ds(first, count)]
+        at[:, :, :, :H] = halves[0].reshape(count, 4, ROWS, H)
+        at[:, :, :, H:] = halves[1].reshape(count, 4, ROWS, H)
+
+    def plus(*terms):
+        return tuple(sum(t[1:], t[0]) for t in zip(*terms))
+
+    for k in ORDER:
+        for half in range(2):
+            load_theirs(half, k).start()
+    for k in ORDER:
+        for half in range(2):
+            load_mine(half, k).start()
+    pl.semaphore_wait(barrier, NZ - 1 + 1 + 6)
     for k in (8, 7, 9, 6, 10, 5, 11, 4, 12, 3, 13, 2, 14, 1, 15):
-        rows_to(k).start()
-    for k in ORDER[1:]:
+        rows_to(k, lambda c: c.start())
+    for k in ORDER:
         for half in range(2):
+            load_theirs(half, k).wait()
+            encode(halves_of(theirs, half, k, 0, 4), asend.at[half, k])
             to_partner(half, k).start()
-            mine(half, k).start()
     own_rows = pltpu.make_async_copy(s_ref.at[z], smat.at[z], s_recv.at[0])
     own_rows.start()
     all_rows = pltpu.make_async_copy(s_ref, srows, stat_sem)
     all_rows.start()
 
-    def b_copy(half, k):
-        return remote(bsend.at[half, k - 1], brecv.at[half, k - 1], b_send.at[half, k - 1], b_recv.at[half, k - 1], along(half, k))
+    def b_copy(kind, half, d):
+        at = (kind, half, d)
+        return remote(bsend.at[at], brecv.at[at], b_send.at[at], b_recv.at[at], along(half, 1 + 2 * d))
+
+    def b_start(kind, half, d, halves):
+        encode(halves, bsend.at[kind, half, d])
+        b_copy(kind, half, d).start()
+
+    def b_get(kind, half, d):
+        b_copy(kind, half, d).wait_recv()
+        return decode(brecv.at[kind, half, d], 8)
 
     def c_copy(half, k):
         return remote(csend.at[half, k - 1], crecv.at[half, k - 1], c_send.at[half, k - 1], c_recv.at[half, k - 1], along(1 - half, k))
@@ -162,13 +204,23 @@
     for k in ORDER:
         for half in range(2):
             to_partner(half, k).wait_recv()
-            mine(half, k).wait()
-            total = own[half, k] + other[half, k]
-            if k:
-                encode(total.reshape(16, ROWS, N), bsend.at[half, k - 1])
-                b_copy(half, k).start()
+            load_mine(half, k).wait()
+            total = plus(halves_of(own, half, k, 0, 4), decode(arecv.at[half, k], 16))
+            low, high = tuple(t[:8] for t in total), tuple(t[8:] for t in total)
+            if k == 2:
+                b_start(0, half, 0, low)
+                b_start(0, half, 1, high)
+            elif k == 1:
+                b_start(1, half, 0, high)
+                put(own, half, 1, 0, 2, low)
+            elif k == 3:
+                b_start(1, half, 1, low)
+                put(own, half, 3, 2, 2, high)
             else:
-                acc[half] = total
+                put(own, half, 0, 0, 4, total)
+    for half in range(2):
+        b_start(2, half, 0, plus(halves_of(own, half, 1, 0, 2), b_get(0, half, 0)))
+        b_start(2, half, 1, plus(halves_of(own, half, 3, 2, 2), b_get(0, half, 1)))
 
     right_z, left_z = column(step(z, 1, NZ)), column(step(z, NZ - 1, NZ))
 
@@ -179,11 +231,12 @@
             sem = (right_sem if d == 0 else left_sem).at[s, p]
             return remote(at, at, sem, recv.at[origin, p], right_z if d == 0 else left_z)
 
-        def arrive(d, s, p, forward):
-            c = hop(d, s, p)
-            c.wait_recv()
-            if forward:
-                c.start()
+        def arrive(d, s, p):
+            if s < 8 or p == d:
+                c = hop(d, s, p)
+                c.wait_recv()
+                if s < 7 or (s == 7 and p == d):
+                    c.start()
 
         def begin():
             for p in range(2):
@@ -192,10 +245,9 @@
 
         def finish():
             for p in range(2):
-                for s in range(8):
-                    hop(0, s, p).wait_send()
-                for s in range(7):
-                    hop(1, s, p).wait_send()
+                for d in range(2):
+                    for s in range(8 if p == d else 7):
+                        hop(d, s, p).wait_send()
 
         return arrive, begin, finish
 
@@ -213,46 +265,27 @@
 
     def plane_sums():
         for half in range(2):
-            left = acc[half, :, :, :, :H].reshape(16, ROWS, H)
-            right = acc[half, :, :, :, H:].reshape(16, ROWS, H)
-            for k in (1, 3, 2):
-                b_copy(half, k).wait_recv()
-                a, b = decode(brecv.at[half, k - 1], 16)
-                left, right = left + a, right + b
-            acc[half, :, :, :, :H] = left.reshape(4, 4, ROWS, H)
-            acc[half, :, :, :, H:] = right.reshape(4, 4, ROWS, H)
+            put(own, half, 0, 0, 2, plus(halves_of(own, half, 0, 0, 2), b_get(1, half, 1), b_get(2, half, 0)))
+            put(own, half, 0, 2, 2, plus(halves_of(own, half, 0, 2, 2), b_get(1, half, 0), b_get(2, half, 1)))
             me = y if half == 0 else x
             for k in (2, 1, 3):
-                encode(acc[half, step(me, k, 4)], csend.at[half, k - 1])
+                encode(halves_of(own, half, 0, step(me, k, 4), 1), csend.at[half, k - 1])
                 c_copy(half, k).start()
-
 
     def own_sums():
         for half in range(2):
             me = y if half == 0 else x
-            g = acc[half, me]
-            left, right = g[:, :, :H], g[:, :, H:]
+            total = halves_of(own, half, 0, me, 1)
             for k in (1, 3, 2):
                 c_copy(half, k).wait_recv()
-                a, b = decode(crecv.at[half, k - 1], 4)
-                left, right = left + a, right + b
-            gown[pl.ds(4 * half, 4), :, :H] = left
-            gown[pl.ds(4 * half, 4), :, H:] = right
-
-    def unpack_g(origin):
-        a, b = decode(gq.at[origin], NB)
-        ah, al = split(a)
-        bh, bl = split(b)
-        ghi[origin, :, :, :H] = ah
-        ghi[origin, :, :, H:] = bh
-        glo[origin, :, :, :H] = al
-        glo[origin, :, :, H:] = bl
+                total = plus(total, decode(crecv.at[half, k - 1], 4))
+            gown[pl.ds(4 * half, 4), :, :H], gown[pl.ds(4 * half, 4), :, H:] = total
+        encode((gown[:, :, :H], gown[:, :, H:]), gq.at[z])
 
     def g_step(s):
         for p in range(2):
-            g_arrive(0, s, p, s < 8)
-            if s < 8:
-                g_arrive(1, s, p, s < 7)
+            g_arrive(0, s, p)
+            g_arrive(1, s, p)
 
     def unpack_step(s):
         unpack_g(step(z, NZ - s, NZ))
@@ -268,9 +301,20 @@
         root[...] = product[N:]
         cur[...] = powered(fs, product[:N], current)
 
+    plane_sums()
+
     own_rows.wait()
     for k in range(1, NZ):
-        rows_from(k).wait_recv()
+        rows_from(k, lambda c: c.wait_recv())
+
+    @pl.when(lax.rem(z, 2) == 0)
+    def _():
+        smat[8:16, :, :H] = smat[0:8, :, H:].reshape(H, H).T.reshape(8, ROWS, H)
+
+    @pl.when(lax.rem(z, 2) == 1)
+    def _():
+        smat[0:8, :, H:] = smat[8:16, :, :H].reshape(H, H).T.reshape(8, ROWS, H)
+
     eye = (lax.broadcasted_iota(I32, (N, N), 0) == lax.broadcasted_iota(I32, (N, N), 1)).astype(F32)
 
     def factor_of(current):
@@ -289,17 +333,15 @@
     fs = split(f)
     cur[...] = powered(fs, dot3(fs, fs), current)
 
-    plane_sums()
     iteration()
     own_sums()
-    encode(gown[...], gq.at[z])
     g_begin()
     iteration()
     iteration()
     g_step(1)
     iteration()
+    iteration()
     g_step(2)
-    iteration()
     last = dot3(split(root[...]), split(factor_of(cur[...])))
     encode_root(last, rq.at[z])
     r_begin()
@@ -307,8 +349,7 @@
     def r_step(s, *units):
         units = units + (None,) * 4
         for i, (p, d) in enumerate(((0, 0), (0, 1), (1, 0), (1, 1))):
-            if s < 8 or d == 0:
-                r_arrive(d, s, p, s < 8 - d)
+            r_arrive(d, s, p)
             if units[i] is not None:
                 units[i]()
 
@@ -381,6 +422,30 @@
     r_step(8, pre(3), None, pre(5))
     precondition(4)
 
+    for half in range(2):
+        for k in range(4):
+            to_partner(half, k).wait_send()
+        for kind in range(3):
+            for d in range(2):
+                b_copy(kind, half, d).wait_send()
+        for k in range(1, 4):
+            c_copy(half, k).wait_send()
+    for k in range(1, NZ):
+        rows_to(k, lambda c: c.wait_send())
+    g_finish()
+    r_finish()
+
+
+def output_kernel(owner_ref, pre_in, new_in, rq, pre_ref, new_ref, kept_ref, sem):
+    dp = lax.axis_index("dp")
+    z = lax.axis_index("owner")
+    copies = [
+        pltpu.make_async_copy(src, dst, sem.at[i])
+        for i, (src, dst) in enumerate(((pre_in, pre_ref), (new_in, new_ref)))
+    ]
+    for copy in copies:
+        copy.start()
+
     first, second, count = jnp.int32(0), jnp.int32(0), jnp.int32(0)
     for j in range(16):
         hit = owner_ref[dp * 16 + j] == z
@@ -395,42 +460,32 @@
         kept_ref[slot, 8:16, :, :H] = (c.T * live).astype(BF16).reshape(8, ROWS, H)
         kept_ref[slot, 8:16, :, H:] = (d * live).astype(BF16).reshape(8, ROWS, H)
 
-    for half in range(2):
-        for k in range(4):
-            to_partner(half, k).wait_send()
-        for k in range(1, 4):
-            b_copy(half, k).wait_send()
-            c_copy(half, k).wait_send()
-    for k in range(1, NZ):
-        rows_to(k).wait_send()
-    g_finish()
-    r_finish()
+    for copy in copies:
+        copy.wait()
 
 
 def shards(partials, statistics, assignment):
     vmem, dma = pltpu.VMEM, pltpu.SemaphoreType.DMA
-    pre, new, kept = pl.pallas_call(
+    in_vmem, in_hbm = pl.BlockSpec(memory_space=pltpu.VMEM), pl.BlockSpec(memory_space=pl.ANY)
+    shapes = (
+        jax.ShapeDtypeStruct((NB, ROWS, N), F32),
+        jax.ShapeDtypeStruct((2 * NB, ROWS, N), F32),
+    )
+    pre, new, rq = pl.pallas_call(
         kernel,
-        out_shape=(
-            jax.ShapeDtypeStruct((NB, ROWS, N), F32),
-            jax.ShapeDtypeStruct((2 * NB, ROWS, N), F32),
-            jax.ShapeDtypeStruct((2, 16, 16, N), BF16),
-        ),
-        in_specs=[
-            pl.BlockSpec(memory_space=pl.ANY),
-            pl.BlockSpec(memory_space=pl.ANY),
-            pl.BlockSpec(memory_space=pltpu.SMEM),
-        ],
-        out_specs=[pl.BlockSpec(memory_space=pltpu.VMEM)] * 3,
+        out_shape=(*shapes, jax.ShapeDtypeStruct((NZ, R_MSG, ROWS, H), I16)),
+        in_specs=[in_hbm] * 2,
+        out_specs=[in_vmem] * 3,
         scratch_shapes=[
             vmem((2 * NB, ROWS, N), F32),
             vmem((2, 4, 4, 4, ROWS, N), F32),
             vmem((2, 4, 4, 4, ROWS, N), F32),
-            vmem((2, 3, B_MSG, ROWS, H), I16),
-            vmem((2, 3, B_MSG, ROWS, H), I16),
+            vmem((2, 4, A_MSG, ROWS, H), I16),
+            vmem((2, 4, A_MSG, ROWS, H), I16),
+            vmem((3, 2, 2, B_MSG, ROWS, H), I16),
+            vmem((3, 2, 2, B_MSG, ROWS, H), I16),
             vmem((2, 3, C_MSG, ROWS, H), I16),
             vmem((2, 3, C_MSG, ROWS, H), I16),
-            vmem((2, 4, 4, ROWS, N), F32),
             vmem((NB, ROWS, N), F32),
             vmem((NZ, ROWS, N), F32),
             vmem((N, N), F32),
@@ -438,22 +493,26 @@
             vmem((NZ, G_MSG, ROWS, H), I16),
             vmem((NZ, NB, ROWS, N), BF16),
             vmem((NZ, NB, ROWS, N), BF16),
-            vmem((NZ, R_MSG, ROWS, H), I16),
-            dma((2, 4)), dma, dma((2, 4)), dma((2, 4)),
-            dma((2, 3)), dma((2, 3)), dma((2, 3)), dma((2, 3)),
+            dma((2, 4)), dma((2, 4)), dma, dma((2, 4)), dma((2, 4)),
+            dma((3, 2, 2)), dma((3, 2, 2)), dma((2, 3)), dma((2, 3)),
             dma((NZ,)), dma((NZ,)),
-            dma((8, 2)), dma((7, 2)), dma((NZ, 2)),
-            dma((8, 2)), dma((7, 2)), dma((NZ, 2)),
+            dma((8, 2)), dma((8, 2)), dma((NZ, 2)),
+            dma((8, 2)), dma((8, 2)), dma((NZ, 2)),
         ],
         compiler_params=pltpu.CompilerParams(
-            collective_id=0, has_side_effects=True, vmem_limit_bytes=60 * 1024 * 1024
+            collective_id=0, has_side_effects=True, vmem_limit_bytes=50 * 1024 * 1024
         ),
         cost_estimate=pl.CostEstimate(flops=3_000_000_000, bytes_accessed=6_000_000, transcendentals=0),
-    )(
-        partials.reshape(NY, NX, 2, NB, ROWS, N),
-        statistics.reshape(2 * NB, ROWS, N),
-        assignment.reshape(-1),
-    )
+    )(partials.reshape(NY, NX, 2, NB, ROWS, N), statistics.reshape(2 * NB, ROWS, N))
+    pre, new, kept = pl.pallas_call(
+        output_kernel,
+        out_shape=(*shapes, jax.ShapeDtypeStruct((2, 16, 16, N), BF16)),
+        in_specs=[pl.BlockSpec(memory_space=pltpu.SMEM)] + [in_vmem] * 3,
+        out_specs=[in_hbm, in_hbm, in_vmem],
+        scratch_shapes=[dma((2,))],
+        compiler_params=pltpu.CompilerParams(vmem_limit_bytes=32 * 1024 * 1024),
+        cost_estimate=pl.CostEstimate(flops=1_000_000, bytes_accessed=1_300_000, transcendentals=0),
+    )(assignment.reshape(-1), pre, new, rq)
     return pre, new.reshape(NB, 2, ROWS, N), kept.reshape(1, 1, 2, N, N)
 
 

time: 94 us -> 85.6 us (0.911); the launches traced: 93.7 us -> 84.4 us
  Pallas kernels: 88.2 us -> 82.8 us
  local copies, waits for them, and re-layouts: 4.91 us -> 0.95 us
    pallas_call x1 -> x2, Pallas kernels: 88.2 us -> 82.8 us  [the longest x1 80.7 us: shards(): pl.pallas_call(kernel, out_shape=(*shapes, jax.ShapeDtypeStruct((NZ, R_MS...]
    unnamed x3 -> x4, local copies, waits for them, and re-layouts: 4.91 us -> 0.95 us
where the time goes in v2:
time: 85.6 us; the launch traced here: 84.4 us
  Pallas kernels  82.8 us (97%)
  local copies, waits for them, and re-layouts  0.95 us (1%)
    pallas_call x1, Pallas kernels, shards(): pl.pallas_call(kernel, out_shape=(*shapes, jax.ShapeDtypeStruct((NZ, R_MS...  80.7 us
    pallas_call x1, Pallas kernels, shards(): pl.pallas_call(output_kernel, out_shape=(*shapes, jax.ShapeDtypeStruct((2...  2.11 us

profile of v2, /device:TPU:24, one launch (start us, length us, event | category | flops | bytes accessed | tf_op | source)
XLA Modules:
  0.0 84.4 jit_solution(11498944747202844931)
XLA Ops:
  0.6 0.0 copy-start.1
  0.6 0.9 %copy-done.1 = f32[8,2,16,256]{3,2,1,0:T(8,128)S(1)} copy-done((f32[8,2,16,256]{3,2,1,0:T(8,128)S(1)}, f32[8,2,16,256]{3,2,1,0:T(8,128)}, u32[]{:S(2)}) %copy-start.1) | copy-done | bytes 262168
  1.6 0.0 copy-start
  1.6 80.7 %shard_map.58 = (f32[8,16,256]{2,1,0:T(8,128)S(1)}, f32[16,16,256]{2,1,0:T(8,128)S(1)}, s16[16,25,16,128]{3,2,1,0:T(8,128)(2,1)S(1)}) custom-call(f32[4,4,2,8,16,256]{5,4,3,2,1,0:T(8,128)} %bitcast.7, f32[16,16,256]{2,1,0:T(8,128)S(1)} %bitcast.6), custom_call_target="tpu_custom_call" | custom-call | flops 3000000000 | bytes 6000000 | tf_op jit(solution)/shard_map/pallas_call | solution.py:474
  82.3 0.0 copy-done
  82.3 2.1 %shard_map.59 = (f32[8,16,256]{2,1,0:T(8,128)}, f32[16,16,256]{2,1,0:T(8,128)}, bf16[2,16,16,256]{3,2,1,0:T(8,128)(2,1)}) custom-call(s32[512]{0:T(512)S(1)} %bitcast.5, f32[8,16,256]{2,1,0:T(8,128)S(1)} %get-tuple-element.9.pre_in, f32[16,16,256]{2,1,0:T(8,128)S(1)} %get-tuple-element.10.new_in, s16[16,25,16,128]{3,2,1,0:T(8,128)(2,1)S(1)} %get-tuple-element.11.rq), custom_call_target="tpu_custom_call" | custom-call | flops 1000000 | bytes 1300000 | tf_op jit(solution)/shard_map/pallas_call | solution.py:507
Async XLA Ops:
  0.6 1.0 %copy-start.1 = (f32[8,2,16,256]{3,2,1,0:T(8,128)S(1)}, f32[8,2,16,256]{3,2,1,0:T(8,128)}, u32[]{:S(2)}) copy-start(f32[8,2,16,256]{3,2,1,0:T(8,128)} %param.4) | copy-start | bytes 786436
  1.6 80.7 %copy-start = (s32[512,1]{0,1:T(1,128)S(1)}, s32[512,1]{0,1:T(1,128)}, u32[]{:S(2)}) copy-start(s32[512,1]{0,1:T(1,128)} %param.5) | copy-start | bytes 6148

commit v3 on v2

--- a/solution.py
+++ b/solution.py
@@ -301,8 +301,6 @@
         root[...] = product[N:]
         cur[...] = powered(fs, product[:N], current)
 
-    plane_sums()
-
     own_rows.wait()
     for k in range(1, NZ):
         rows_from(k, lambda c: c.wait_recv())
@@ -333,6 +331,7 @@
     fs = split(f)
     cur[...] = powered(fs, dot3(fs, fs), current)
 
+    plane_sums()
     iteration()
     own_sums()
     g_begin()
@@ -355,12 +354,12 @@
 
     unpack_g(z)
     unpack_step(1)
-    for s in range(1, 4):
-        g_step(2 * s + 1)
-        unpack_step(2 * s)
+    for s in range(1, 6):
+        g_step(s + 2)
+        unpack_step(s + 1)
         r_step(s)
-        g_step(2 * s + 2)
-        unpack_step(2 * s + 1)
+    g_step(8)
+    unpack_step(7)
     unpack_step(8)
     all_rows.wait()
 
@@ -415,11 +414,11 @@
     def pre(t):
         return lambda: precondition(t)
 
-    r_step(4, stat(0), stat(1), pre(0), stat(2))
-    r_step(5, stat(3), pre(1), stat(4), pre(7))
-    r_step(6, stat(5), pre(2), stat(6), pre(6))
-    r_step(7, stat(7))
-    r_step(8, pre(3), None, pre(5))
+    r_step(6, stat(0), stat(1), stat(2), stat(3))
+    r_step(7, stat(4), stat(5), stat(6), stat(7))
+    for t in (0, 1, 7, 2, 6, 3, 5):
+        precondition(t)
+    r_step(8)
     precondition(4)
 
     for half in range(2):

time: 85.6 us -> 82.2 us (0.960); the launches traced: 84.4 us -> 82.1 us
  Pallas kernels: 82.8 us -> 80.5 us
    pallas_call x1, Pallas kernels: 80.7 us -> 78.4 us  [shards(): pl.pallas_call(kernel, out_shape=(*shapes, jax.ShapeDtypeStruct((NZ, R_MS...]
where the time goes in v3:
time: 82.2 us; the launch traced here: 82.1 us
  Pallas kernels  80.5 us (98%)
  local copies, waits for them, and re-layouts  0.95 us (1%)
    pallas_call x1, Pallas kernels, shards(): pl.pallas_call(kernel, out_shape=(*shapes, jax.ShapeDtypeStruct((NZ, R_MS...  78.4 us
    pallas_call x1, Pallas kernels, shards(): pl.pallas_call(output_kernel, out_shape=(*shapes, jax.ShapeDtypeStruct((2...  2.11 us

profile of v3, /device:TPU:24, one launch (start us, length us, event | category | flops | bytes accessed | tf_op | source)
XLA Modules:
  0.0 82.1 jit_solution(16071263257826053074)
XLA Ops:
  0.6 0.0 copy-start.1
  0.6 0.9 %copy-done.1 = f32[8,2,16,256]{3,2,1,0:T(8,128)S(1)} copy-done((f32[8,2,16,256]{3,2,1,0:T(8,128)S(1)}, f32[8,2,16,256]{3,2,1,0:T(8,128)}, u32[]{:S(2)}) %copy-start.1) | copy-done | bytes 262168
  1.6 0.0 copy-start
  1.6 78.4 %shard_map.58 = (f32[8,16,256]{2,1,0:T(8,128)S(1)}, f32[16,16,256]{2,1,0:T(8,128)S(1)}, s16[16,25,16,128]{3,2,1,0:T(8,128)(2,1)S(1)}) custom-call(f32[4,4,2,8,16,256]{5,4,3,2,1,0:T(8,128)} %bitcast.7, f32[16,16,256]{2,1,0:T(8,128)S(1)} %bitcast.6), custom_call_target="tpu_custom_call" | custom-call | flops 3000000000 | bytes 6000000 | tf_op jit(solution)/shard_map/pallas_call | solution.py:473
  80.0 0.0 copy-done
  80.0 2.1 %shard_map.59 = (f32[8,16,256]{2,1,0:T(8,128)}, f32[16,16,256]{2,1,0:T(8,128)}, bf16[2,16,16,256]{3,2,1,0:T(8,128)(2,1)}) custom-call(s32[512]{0:T(512)S(1)} %bitcast.5, f32[8,16,256]{2,1,0:T(8,128)S(1)} %get-tuple-element.9.pre_in, f32[16,16,256]{2,1,0:T(8,128)S(1)} %get-tuple-element.10.new_in, s16[16,25,16,128]{3,2,1,0:T(8,128)(2,1)S(1)} %get-tuple-element.11.rq), custom_call_target="tpu_custom_call" | custom-call | flops 1000000 | bytes 1300000 | tf_op jit(solution)/shard_map/pallas_call | solution.py:506
Async XLA Ops:
  0.6 1.0 %copy-start.1 = (f32[8,2,16,256]{3,2,1,0:T(8,128)S(1)}, f32[8,2,16,256]{3,2,1,0:T(8,128)}, u32[]{:S(2)}) copy-start(f32[8,2,16,256]{3,2,1,0:T(8,128)} %param.4) | copy-start | bytes 786436
  1.6 78.4 %copy-start = (s32[512,1]{0,1:T(1,128)S(1)}, s32[512,1]{0,1:T(1,128)}, u32[]{:S(2)}) copy-start(s32[512,1]{0,1:T(1,128)} %param.5) | copy-start | bytes 6148

commit v4 on v3

--- a/solution.py
+++ b/solution.py
@@ -15,9 +15,9 @@
 H = 128
 ITERS = 7
 LEVELS = 32760.0 / 32768.0
-A_MSG, B_MSG, C_MSG, G_MSG, R_MSG = 33, 17, 9, 17, 25
+A_MSG, B_MSG, C_MSG, G_MSG, R_MSG = 33, 17, 9, 17, 18
 G_PARTS = ((0, 9), (9, 8))
-R_PARTS = ((0, 13), (13, 12))
+R_PARTS = ((0, 9), (9, 9))
 
 
 def code(x):
@@ -48,16 +48,32 @@
     return value(src[0:m]) * down, value(src[m : 2 * m]) * down
 
 
+def square_iota():
+    return lax.broadcasted_iota(I32, (H, H), 0), lax.broadcasted_iota(I32, (H, H), 1)
+
+
 def encode_root(x, dst):
-    x = jnp.concatenate([x[:H, :H], x[:H, H:], x[H:, H:]], axis=0).reshape(24, ROWS, H)
+    row, col = square_iota()
+    last = x[H:, H:]
+    folded = jnp.where(row <= col, x[:H, :H], last)
+    diagonal = jnp.sum(jnp.where(row == col, last, 0.0), axis=0, keepdims=True)
+    diagonal = jnp.where(row[:ROWS] == 0, diagonal, 0.0)
+    x = jnp.concatenate([folded, x[:H, H:], diagonal], axis=0).reshape(17, ROWS, H)
     e = jnp.ceil(jnp.log2(jnp.maximum(jnp.max(jnp.abs(x), axis=0), 1e-30)))
-    dst[0:24] = code(x * (jnp.exp2(15.0 - e) * LEVELS)[None])
-    dst[24] = code(e)
+    dst[0:17] = code(x * (jnp.exp2(15.0 - e) * LEVELS)[None])
+    dst[17] = code(e)
 
 
 def decode_root(q):
-    v = (value(q[0:24]) * unit(q[24])[None]).reshape(3 * H, H)
-    return v[:H], v[H : 2 * H], v[2 * H :]
+    v = value(q[0:17]) * unit(q[17])[None]
+    folded, upper, diagonal = v[0:8].reshape(H, H), v[8:16].reshape(H, H), v[16][0:1]
+    row, col = square_iota()
+    turned = folded.T
+    return (
+        jnp.where(row <= col, folded, turned),
+        upper,
+        jnp.where(row > col, folded, jnp.where(row == col, diagonal, turned)),
+    )
 
 
 def split(x):
@@ -380,20 +396,24 @@
         three = dot(jnp.concatenate([ch, cl], axis=0), gh)
         new_ref[2 * b + 1] = srows[2 * b + 1] + three[:16] + (three[16:32] + dot(ch, gl))
 
-    pick_low = (
-        lax.broadcasted_iota(I32, (ROWS, H), 1)
-        == lax.broadcasted_iota(I32, (ROWS, H), 0) + (z - 8) * ROWS
-    ).astype(F32).astype(BF16)
+    z8 = lax.rem(z, 8)
+    line = lax.broadcasted_iota(I32, (ROWS, H), 0) + z8 * ROWS
+    lane = lax.broadcasted_iota(I32, (ROWS, H), 1)
+    pick_in = (lane == line).astype(F32).astype(BF16)
 
     def precondition(t):
         b = step(pair, t, NB)
         gh, gl = halves(b)
         q = rq[2 * b]
-        down = unit(q[24])
-        bh, bl = split((value(q[8:16]) * down[None]).reshape(H, H))
-        upper = value(rq[2 * b, lax.rem(z, 8)]) * down
-        lower = dot_nt(pick_low, bh) + dot_nt(pick_low, bl)
-        rows = jnp.concatenate([jnp.where(z < 8, upper, lower), value(rq[2 * b, 8 + z]) * down], axis=1)
+        down = unit(q[17])
+        high, low = split((value(q[0:16]) * down[None]).reshape(2 * H, H))
+        turned = dot_nt(pick_in, high) + dot_nt(pick_in, low)
+        folded = value(rq[2 * b, z8]) * down
+        upper = value(rq[2 * b, 8 + z8]) * down
+        diagonal = (value(q[16]) * down)[0:1]
+        first = jnp.concatenate([jnp.where(line <= lane, folded, turned[:, :H]), upper], axis=1)
+        second = jnp.where(line > lane, folded, jnp.where(line == lane, diagonal, turned[:, :H]))
+        rows = jnp.where(z < 8, first, jnp.concatenate([turned[:, H:], second], axis=1))
         lh, ll = split(rows)
         shaped = dot(jnp.concatenate([lh, ll], axis=0), gh)
         shaped = shaped[:16] + (shaped[16:] + dot(lh, gl))

time: 82.2 us -> 79.9 us (0.972)
  Pallas kernels: 80.5 us -> 77.9 us
    pallas_call x1, Pallas kernels: 78.4 us -> 75.8 us  [shards(): pl.pallas_call(kernel, out_shape=(*shapes, jax.ShapeDtypeStruct((NZ, R_MS...]
where the time goes in v4:
time: 79.9 us; the launch traced here: 79.5 us
  Pallas kernels  77.9 us (97%)
  local copies, waits for them, and re-layouts  0.95 us (1%)
    pallas_call x1, Pallas kernels, shards(): pl.pallas_call(kernel, out_shape=(*shapes, jax.ShapeDtypeStruct((NZ, R_MS...  75.8 us
    pallas_call x1, Pallas kernels, shards(): pl.pallas_call(output_kernel, out_shape=(*shapes, jax.ShapeDtypeStruct((2...  2.1 us

profile of v4, /device:TPU:24, one launch (start us, length us, event | category | flops | bytes accessed | tf_op | source)
XLA Modules:
  0.0 79.5 jit_solution(2066327712568631159)
XLA Ops:
  0.6 0.0 copy-start.1
  0.6 0.9 %copy-done.1 = f32[8,2,16,256]{3,2,1,0:T(8,128)S(1)} copy-done((f32[8,2,16,256]{3,2,1,0:T(8,128)S(1)}, f32[8,2,16,256]{3,2,1,0:T(8,128)}, u32[]{:S(2)}) %copy-start.1) | copy-done | bytes 262168
  1.6 0.0 copy-start
  1.6 75.8 %shard_map.58 = (f32[8,16,256]{2,1,0:T(8,128)S(1)}, f32[16,16,256]{2,1,0:T(8,128)S(1)}, s16[16,18,16,128]{3,2,1,0:T(8,128)(2,1)S(1)}) custom-call(f32[4,4,2,8,16,256]{5,4,3,2,1,0:T(8,128)} %bitcast.7, f32[16,16,256]{2,1,0:T(8,128)S(1)} %bitcast.6), custom_call_target="tpu_custom_call" | custom-call | flops 3000000000 | bytes 6000000 | tf_op jit(solution)/shard_map/pallas_call | solution.py:493
  77.4 0.0 copy-done
  77.4 2.1 %shard_map.59 = (f32[8,16,256]{2,1,0:T(8,128)}, f32[16,16,256]{2,1,0:T(8,128)}, bf16[2,16,16,256]{3,2,1,0:T(8,128)(2,1)}) custom-call(s32[512]{0:T(512)S(1)} %bitcast.5, f32[8,16,256]{2,1,0:T(8,128)S(1)} %get-tuple-element.9.pre_in, f32[16,16,256]{2,1,0:T(8,128)S(1)} %get-tuple-element.10.new_in, s16[16,18,16,128]{3,2,1,0:T(8,128)(2,1)S(1)} %get-tuple-element.11.rq), custom_call_target="tpu_custom_call" | custom-call | flops 1000000 | bytes 1300000 | tf_op jit(solution)/shard_map/pallas_call | solution.py:526
Async XLA Ops:
  0.6 1.0 %copy-start.1 = (f32[8,2,16,256]{3,2,1,0:T(8,128)S(1)}, f32[8,2,16,256]{3,2,1,0:T(8,128)}, u32[]{:S(2)}) copy-start(f32[8,2,16,256]{3,2,1,0:T(8,128)} %param.4) | copy-start | bytes 786436
  1.6 75.8 %copy-start = (s32[512,1]{0,1:T(1,128)S(1)}, s32[512,1]{0,1:T(1,128)}, u32[]{:S(2)}) copy-start(s32[512,1]{0,1:T(1,128)} %param.5) | copy-start | bytes 6148

commit v5 on v4

--- a/solution.py
+++ b/solution.py
@@ -15,7 +15,7 @@
 H = 128
 ITERS = 7
 LEVELS = 32760.0 / 32768.0
-A_MSG, B_MSG, C_MSG, G_MSG, R_MSG = 33, 17, 9, 17, 18
+B_MSG, C_MSG, G_MSG, R_MSG = 17, 9, 17, 18
 G_PARTS = ((0, 9), (9, 8))
 R_PARTS = ((0, 9), (9, 9))
 
@@ -96,7 +96,7 @@
 
 def kernel(
     p_ref, s_ref, pre_ref, new_ref, rq,
-    srows, own, theirs, asend, arecv, bsend, brecv, csend, crecv, gown, smat, cur, root, gq, ghi, glo,
+    srows, own, theirs, other, bsend, brecv, csend, crecv, gown, smat, cur, root, gq, ghi, glo,
     own_sem, their_sem, stat_sem, a_send, a_recv, b_send, b_recv, c_send, c_recv, s_send, s_recv,
     g_right, g_left, g_recv, r_right, r_left, r_recv,
 ):
@@ -139,7 +139,7 @@
         return p_ref.at[step(y, k, NY), :, cc, pl.ds(4, 4)]
 
     def to_partner(half, k):
-        return remote(asend.at[half, k], arecv.at[half, k], a_send.at[half, k], a_recv.at[half, k], partner)
+        return remote(theirs.at[half, k], other.at[half, k], a_send.at[half, k], a_recv.at[half, k], partner)
 
     def load(half, k, cc, dst, sem):
         return pltpu.make_async_copy(chunk(half, k, cc), dst.at[half, k], sem.at[half, k])
@@ -190,13 +190,16 @@
         for half in range(2):
             load_mine(half, k).start()
     pl.semaphore_wait(barrier, NZ - 1 + 1 + 6)
+    def send_share(k):
+        for half in range(2):
+            load_theirs(half, k).wait()
+            to_partner(half, k).start()
+
+    send_share(2)
     for k in (8, 7, 9, 6, 10, 5, 11, 4, 12, 3, 13, 2, 14, 1, 15):
         rows_to(k, lambda c: c.start())
-    for k in ORDER:
-        for half in range(2):
-            load_theirs(half, k).wait()
-            encode(halves_of(theirs, half, k, 0, 4), asend.at[half, k])
-            to_partner(half, k).start()
+    for k in ORDER[1:]:
+        send_share(k)
     own_rows = pltpu.make_async_copy(s_ref.at[z], smat.at[z], s_recv.at[0])
     own_rows.start()
     all_rows = pltpu.make_async_copy(s_ref, srows, stat_sem)
@@ -221,7 +224,7 @@
         for half in range(2):
             to_partner(half, k).wait_recv()
             load_mine(half, k).wait()
-            total = plus(halves_of(own, half, k, 0, 4), decode(arecv.at[half, k], 16))
+            total = plus(halves_of(own, half, k, 0, 4), halves_of(other, half, k, 0, 4))
             low, high = tuple(t[:8] for t in total), tuple(t[8:] for t in total)
             if k == 2:
                 b_start(0, half, 0, low)
@@ -259,11 +262,12 @@
                 for d in range(2):
                     hop(d, 0, p).start()
 
-        def finish():
-            for p in range(2):
-                for d in range(2):
-                    for s in range(8 if p == d else 7):
-                        hop(d, s, p).wait_send()
+        def finish(steps):
+            for s in steps:
+                for p in range(2):
+                    for d in range(2):
+                        if s < 7 or p == d:
+                            hop(d, s, p).wait_send()
 
         return arrive, begin, finish
 
@@ -368,12 +372,26 @@
             if units[i] is not None:
                 units[i]()
 
+    def early_sends():
+        for half in range(2):
+            for k in range(4):
+                to_partner(half, k).wait_send()
+            for kind in range(3):
+                for d in range(2):
+                    b_copy(kind, half, d).wait_send()
+            for k in range(1, 4):
+                c_copy(half, k).wait_send()
+        for k in range(1, NZ):
+            rows_to(k, lambda c: c.wait_send())
+
     unpack_g(z)
     unpack_step(1)
     for s in range(1, 6):
         g_step(s + 2)
         unpack_step(s + 1)
         r_step(s)
+        if s == 2:
+            early_sends()
     g_step(8)
     unpack_step(7)
     unpack_step(8)
@@ -438,21 +456,11 @@
     r_step(7, stat(4), stat(5), stat(6), stat(7))
     for t in (0, 1, 7, 2, 6, 3, 5):
         precondition(t)
+    g_finish(range(8))
+    r_finish(range(6))
     r_step(8)
     precondition(4)
-
-    for half in range(2):
-        for k in range(4):
-            to_partner(half, k).wait_send()
-        for kind in range(3):
-            for d in range(2):
-                b_copy(kind, half, d).wait_send()
-        for k in range(1, 4):
-            c_copy(half, k).wait_send()
-    for k in range(1, NZ):
-        rows_to(k, lambda c: c.wait_send())
-    g_finish()
-    r_finish()
+    r_finish((6, 7))
 
 
 def output_kernel(owner_ref, pre_in, new_in, rq, pre_ref, new_ref, kept_ref, sem):
@@ -499,8 +507,7 @@
             vmem((2 * NB, ROWS, N), F32),
             vmem((2, 4, 4, 4, ROWS, N), F32),
             vmem((2, 4, 4, 4, ROWS, N), F32),
-            vmem((2, 4, A_MSG, ROWS, H), I16),
-            vmem((2, 4, A_MSG, ROWS, H), I16),
+            vmem((2, 4, 4, 4, ROWS, N), F32),
             vmem((3, 2, 2, B_MSG, ROWS, H), I16),
             vmem((3, 2, 2, B_MSG, ROWS, H), I16),
             vmem((2, 3, C_MSG, ROWS, H), I16),

time: 79.9 us -> 79.5 us (level)
  no operation moved by 1% of the time
where the time goes in v5:
time: 79.5 us; the launch traced here: 79.4 us
  Pallas kernels  77.8 us (98%)
  local copies, waits for them, and re-layouts  0.95 us (1%)
    pallas_call x1, Pallas kernels, shards(): pl.pallas_call(kernel, out_shape=(*shapes, jax.ShapeDtypeStruct((NZ, R_MS...  75.7 us
    pallas_call x1, Pallas kernels, shards(): pl.pallas_call(output_kernel, out_shape=(*shapes, jax.ShapeDtypeStruct((2...  2.1 us

profile of v5, /device:TPU:24, one launch (start us, length us, event | category | flops | bytes accessed | tf_op | source)
XLA Modules:
  0.0 79.4 jit_solution(12231222705951017696)
XLA Ops:
  0.6 0.0 copy-start.1
  0.6 0.9 %copy-done.1 = f32[8,2,16,256]{3,2,1,0:T(8,128)S(1)} copy-done((f32[8,2,16,256]{3,2,1,0:T(8,128)S(1)}, f32[8,2,16,256]{3,2,1,0:T(8,128)}, u32[]{:S(2)}) %copy-start.1) | copy-done | bytes 262168
  1.6 0.0 copy-start
  1.6 75.7 %shard_map.58 = (f32[8,16,256]{2,1,0:T(8,128)S(1)}, f32[16,16,256]{2,1,0:T(8,128)S(1)}, s16[16,18,16,128]{3,2,1,0:T(8,128)(2,1)S(1)}) custom-call(f32[4,4,2,8,16,256]{5,4,3,2,1,0:T(8,128)} %bitcast.7, f32[16,16,256]{2,1,0:T(8,128)S(1)} %bitcast.6), custom_call_target="tpu_custom_call" | custom-call | flops 3000000000 | bytes 6000000 | tf_op jit(solution)/shard_map/pallas_call | solution.py:501
  77.3 0.0 copy-done
  77.3 2.1 %shard_map.59 = (f32[8,16,256]{2,1,0:T(8,128)}, f32[16,16,256]{2,1,0:T(8,128)}, bf16[2,16,16,256]{3,2,1,0:T(8,128)(2,1)}) custom-call(s32[512]{0:T(512)S(1)} %bitcast.5, f32[8,16,256]{2,1,0:T(8,128)S(1)} %get-tuple-element.9.pre_in, f32[16,16,256]{2,1,0:T(8,128)S(1)} %get-tuple-element.10.new_in, s16[16,18,16,128]{3,2,1,0:T(8,128)(2,1)S(1)} %get-tuple-element.11.rq), custom_call_target="tpu_custom_call" | custom-call | flops 1000000 | bytes 1300000 | tf_op jit(solution)/shard_map/pallas_call | solution.py:533
Async XLA Ops:
  0.6 1.0 %copy-start.1 = (f32[8,2,16,256]{3,2,1,0:T(8,128)S(1)}, f32[8,2,16,256]{3,2,1,0:T(8,128)}, u32[]{:S(2)}) copy-start(f32[8,2,16,256]{3,2,1,0:T(8,128)} %param.4) | copy-start | bytes 786436
  1.6 75.7 %copy-start = (s32[512,1]{0,1:T(1,128)S(1)}, s32[512,1]{0,1:T(1,128)}, u32[]{:S(2)}) copy-start(s32[512,1]{0,1:T(1,128)} %param.5) | copy-start | bytes 6148

commit v6 on v5

--- a/solution.py
+++ b/solution.py
@@ -16,8 +16,8 @@
 ITERS = 7
 LEVELS = 32760.0 / 32768.0
 B_MSG, C_MSG, G_MSG, R_MSG = 17, 9, 17, 18
-G_PARTS = ((0, 9), (9, 8))
-R_PARTS = ((0, 9), (9, 9))
+G_PARTS = ((0, 6), (6, 6), (12, 5))
+R_PARTS = ((0, 6), (6, 6), (12, 6))
 
 
 def code(x):
@@ -247,26 +247,26 @@
         def hop(d, s, p):
             origin = step(z, NZ - s, NZ) if d == 0 else step(z, s, NZ)
             at = buf.at[origin, pl.ds(*parts[p])]
-            sem = (right_sem if d == 0 else left_sem).at[s, p]
+            sem = (right_sem if d == 0 else left_sem).at[s % 8, p]
             return remote(at, at, sem, recv.at[origin, p], right_z if d == 0 else left_z)
 
         def arrive(d, s, p):
-            if s < 8 or p == d:
+            if s < 8 or p // 2 == d:
                 c = hop(d, s, p)
                 c.wait_recv()
-                if s < 7 or (s == 7 and p == d):
+                if s < 7 or (s == 7 and p // 2 == d):
                     c.start()
 
         def begin():
-            for p in range(2):
+            for p in range(3):
                 for d in range(2):
                     hop(d, 0, p).start()
 
         def finish(steps):
             for s in steps:
-                for p in range(2):
+                for p in range(3):
                     for d in range(2):
-                        if s < 7 or p == d:
+                        if s < 7 or p // 2 == d:
                             hop(d, s, p).wait_send()
 
         return arrive, begin, finish
@@ -303,7 +303,7 @@
         encode((gown[:, :, :H], gown[:, :, H:]), gq.at[z])
 
     def g_step(s):
-        for p in range(2):
+        for p in range(3):
             g_arrive(0, s, p)
             g_arrive(1, s, p)
 
@@ -366,8 +366,8 @@
     r_begin()
 
     def r_step(s, *units):
-        units = units + (None,) * 4
-        for i, (p, d) in enumerate(((0, 0), (0, 1), (1, 0), (1, 1))):
+        units = units + (None,) * 6
+        for i, (p, d) in enumerate(((0, 0), (0, 1), (1, 0), (1, 1), (2, 0), (2, 1))):
             r_arrive(d, s, p)
             if units[i] is not None:
                 units[i]()
@@ -522,8 +522,8 @@
             dma((2, 4)), dma((2, 4)), dma, dma((2, 4)), dma((2, 4)),
             dma((3, 2, 2)), dma((3, 2, 2)), dma((2, 3)), dma((2, 3)),
             dma((NZ,)), dma((NZ,)),
-            dma((8, 2)), dma((8, 2)), dma((NZ, 2)),
-            dma((8, 2)), dma((8, 2)), dma((NZ, 2)),
+            dma((8, 3)), dma((8, 3)), dma((NZ, 3)),
+            dma((8, 3)), dma((8, 3)), dma((NZ, 3)),
         ],
         compiler_params=pltpu.CompilerParams(
             collective_id=0, has_side_effects=True, vmem_limit_bytes=50 * 1024 * 1024

time: 79.5 us -> 79.5 us (level)
  no operation moved by 1% of the time
where the time goes in v6:
time: 79.5 us; the launch traced here: 79.3 us
  Pallas kernels  77.7 us (98%)
  local copies, waits for them, and re-layouts  0.95 us (1%)
    pallas_call x1, Pallas kernels, shards(): pl.pallas_call(kernel, out_shape=(*shapes, jax.ShapeDtypeStruct((NZ, R_MS...  75.6 us
    pallas_call x1, Pallas kernels, shards(): pl.pallas_call(output_kernel, out_shape=(*shapes, jax.ShapeDtypeStruct((2...  2.1 us

profile of v6, /device:TPU:24, one launch (start us, length us, event | category | flops | bytes accessed | tf_op | source)
XLA Modules:
  0.0 79.3 jit_solution(7883492398682605474)
XLA Ops:
  0.6 0.0 copy-start.1
  0.6 0.9 %copy-done.1 = f32[8,2,16,256]{3,2,1,0:T(8,128)S(1)} copy-done((f32[8,2,16,256]{3,2,1,0:T(8,128)S(1)}, f32[8,2,16,256]{3,2,1,0:T(8,128)}, u32[]{:S(2)}) %copy-start.1) | copy-done | bytes 262168
  1.6 0.0 copy-start
  1.6 75.6 %shard_map.58 = (f32[8,16,256]{2,1,0:T(8,128)S(1)}, f32[16,16,256]{2,1,0:T(8,128)S(1)}, s16[16,18,16,128]{3,2,1,0:T(8,128)(2,1)S(1)}) custom-call(f32[4,4,2,8,16,256]{5,4,3,2,1,0:T(8,128)} %bitcast.7, f32[16,16,256]{2,1,0:T(8,128)S(1)} %bitcast.6), custom_call_target="tpu_custom_call" | custom-call | flops 3000000000 | bytes 6000000 | tf_op jit(solution)/shard_map/pallas_call | solution.py:501
  77.2 0.0 copy-done
  77.2 2.1 %shard_map.59 = (f32[8,16,256]{2,1,0:T(8,128)}, f32[16,16,256]{2,1,0:T(8,128)}, bf16[2,16,16,256]{3,2,1,0:T(8,128)(2,1)}) custom-call(s32[512]{0:T(512)S(1)} %bitcast.5, f32[8,16,256]{2,1,0:T(8,128)S(1)} %get-tuple-element.9.pre_in, f32[16,16,256]{2,1,0:T(8,128)S(1)} %get-tuple-element.10.new_in, s16[16,18,16,128]{3,2,1,0:T(8,128)(2,1)S(1)} %get-tuple-element.11.rq), custom_call_target="tpu_custom_call" | custom-call | flops 1000000 | bytes 1300000 | tf_op jit(solution)/shard_map/pallas_call | solution.py:533
Async XLA Ops:
  0.6 1.0 %copy-start.1 = (f32[8,2,16,256]{3,2,1,0:T(8,128)S(1)}, f32[8,2,16,256]{3,2,1,0:T(8,128)}, u32[]{:S(2)}) copy-start(f32[8,2,16,256]{3,2,1,0:T(8,128)} %param.4) | copy-start | bytes 786436
  1.6 75.6 %copy-start = (s32[512,1]{0,1:T(1,128)S(1)}, s32[512,1]{0,1:T(1,128)}, u32[]{:S(2)}) copy-start(s32[512,1]{0,1:T(1,128)} %param.5) | copy-start | bytes 6148
